TPU v7x, 32 devices: a whole 2x2x4 slice. The times are simulated.
32 devices in a mesh: grp: 2 (over y), ra: 16 (over z, x, core).
Axes of the slice: x: 2, y: 2, z: 4, core: 2. Of those that a mesh axis runs over, the one named last changes fastest.
Arguments:
- split_maps: bfloat16 [4, 3, 1024, 2048], P(None, None, 'grp', 'ra'), parts along dimension 2, may hold values from -6 to 6
- tile_start: int32 [32, 2], P(('grp', 'ra')), parts along dimension 0, may hold values from 0 to 31, as said below
- pattern: int32 [32, 256], P('grp', 'ra'), parts along dimension 0, may hold values 0 or 1
Outputs:
- noise_model: float32 [32, 256, 6, 256], P('grp', 'ra'), parts along dimension 0
There are 2 independent parts, one for each index of `grp`. A program takes and returns all parts, laid end to end along the dimension named above; each array names one. Nothing has to cross between parts.
Inputs may be any that keep to these rules, and one draw needn't show every extreme that they name: `tile_start`: tile t belongs to the device of index t // 1 along ra. Its first block row lies from 0 to 4. Its first block column, taken relative to 2 t (the first block column of its owner's strip) around the wrapping map, lies from -2 to 0; both ends are reached. A tile covers 4 by 4 blocks.
All inputs are finite; a program needn't handle non-finite values. No bound on the sum of `pattern` on one device may be relied on, other than what follows from the above.
Results may differ from a plain program's by a relative error of at most 0.0024.
Values may be sent and summed in bfloat16 or wider, within the bound.
A program may use at most 192 MiB of HBM per device.

v0:
```python
import math

import jax
import jax.numpy as jnp
from jax import lax
from jax.sharding import PartitionSpec as P

SPLITS = 4
STOKES = 3
BPX = 64
CBD = 2
REACH = 1
FBN = 16
TILE = 256
FBS = 16
FBLK = 256


cov_pairs = ((0, 0), (1, 1), (2, 2), (0, 1), (0, 2), (1, 2))


def with_halo(shard, sides, width):
    for axis, dim in sides:
        size, length = (lax.axis_size(axis), shard.shape[dim])
        up = [(i, (i + 1) % size) for i in range(size)]
        down = [(j, i) for i, j in up]
        last = lax.slice_in_dim(shard, length - width, length, axis=dim)
        initial = lax.slice_in_dim(shard, 0, width, axis=dim)
        before = lax.ppermute(last, axis, up)
        after = lax.ppermute(initial, axis, down)
        shard = jnp.concatenate([before, shard, after], axis=dim)
    return shard


def fourier_tables(length):
    counter = jnp.arange(length, dtype=jnp.int32)
    phase = counter[:, None] * counter[None, :] % length
    angle = 2.0 * math.pi / length * phase.astype(jnp.float32)
    factor = 1.0 / math.sqrt(length)
    return (
        (jnp.cos(angle) * factor).astype(jnp.bfloat16),
        (jnp.sin(angle) * factor).astype(jnp.bfloat16),
    )


def taper_table(length):
    edge = length // 8
    counter = jnp.arange(length, dtype=jnp.float32)
    rising = jnp.where(counter < edge, jnp.sin(math.pi * (counter + 0.5) / (2 * edge)) ** 2, 1.0)
    line = rising * rising[::-1]
    return line[:, None] * line[None, :]


def blockify(spectra):
    count = spectra.shape[0]
    shaped = spectra.reshape(count, FBN, FBS, FBN, FBS)
    return shaped.transpose(1, 3, 0, 2, 4).reshape(FBN * FBN, count, FBS * FBS)


def cross_power(stacked):
    values = stacked.astype(jnp.float32)
    real_part = values[..., 0, :, :, :]
    imag_part = values[..., 1, :, :, :]
    terms = []
    for first_axis, second_axis in cov_pairs:
        product = (
            real_part[..., first_axis, :] * real_part[..., second_axis, :]
            + imag_part[..., first_axis, :] * imag_part[..., second_axis, :]
        )
        terms.append(jnp.mean(product, axis=-2))
    return jnp.stack(terms, axis=-2)


def body(split_maps, tile_start, pattern):
    width = REACH * CBD * BPX
    window = with_halo(split_maps, (("ra", 3),), width)
    first_block = (lax.axis_index("ra") - REACH) * CBD
    total_blocks = CBD * lax.axis_size("ra")
    taper = taper_table(TILE)
    cosine, sine = fourier_tables(TILE)
    section_one = jnp.concatenate([cosine, sine], axis=1)
    section_two = jnp.concatenate([cosine, sine], axis=0)
    zero_index = jnp.zeros((), jnp.int32)

    def one_split(stokes_maps):
        flat = stokes_maps.reshape(STOKES * TILE, TILE)
        halfway = jnp.dot(flat, section_one, preferred_element_type=jnp.float32).astype(
            jnp.bfloat16
        )
        halfway = halfway.reshape(STOKES, TILE, 2 * TILE)
        outer = jnp.einsum("ky,mya->mka", section_two, halfway, preferred_element_type=jnp.float32)
        real_part = (outer[:, :TILE, :TILE] - outer[:, TILE:, TILE:]).astype(jnp.bfloat16)
        imag_part = (outer[:, :TILE, TILE:] + outer[:, TILE:, :TILE]).astype(jnp.bfloat16)
        return (real_part, imag_part)

    def one_tile(corner):
        local_column = (corner[1] - first_block) % total_blocks * BPX
        row_start = corner[0] * BPX
        tile_pixels = lax.dynamic_slice(
            window, (zero_index, zero_index, row_start, local_column), (SPLITS, STOKES, TILE, TILE)
        )
        values = tile_pixels.astype(jnp.float32)
        difference = values - jnp.mean(values, axis=0, keepdims=True)
        tapered = (difference * taper).astype(jnp.bfloat16)
        real_part, imag_part = lax.map(one_split, tapered)
        spectra = jnp.concatenate(
            [
                real_part.reshape(SPLITS * STOKES, TILE, TILE),
                imag_part.reshape(SPLITS * STOKES, TILE, TILE),
            ],
            axis=0,
        )
        return blockify(spectra)

    spectra_blocks = lax.map(one_tile, tile_start)
    owned = spectra_blocks.shape[0]
    local_cross = cross_power(spectra_blocks.reshape(owned, FBLK, 2, SPLITS, STOKES, FBS * FBS))
    cross = lax.all_to_all(local_cross, "ra", split_axis=1, concat_axis=0, tiled=True)
    block_mean = jnp.mean(cross, axis=-1, keepdims=True)
    level = jnp.mean(block_mean, axis=0, keepdims=True)
    kept = jnp.where((pattern == 1)[:, :, None, None], cross, block_mean)
    return 0.5 * kept + 0.5 * level


def solution(mesh):
    placed = (P(None, None, "grp", "ra"), P(("grp", "ra"), None), P("grp", "ra"))
    return jax.shard_map(
        body, mesh=mesh, in_specs=placed, out_specs=P("grp", "ra", None, None), check_vma=False
    )
```

profile of v0, /device:TPU:15, one launch (start us, length us, event | category | flops | bytes accessed | tf_op | source)
XLA Modules:
  0.0 229.8 jit_solution(1735479062502306508)
XLA Ops:
  0.0 0.0 copy-start.1
  0.0 1.8 collective-permute-start
  1.8 0.0 collective-permute-start.1
  1.8 1.3 fusion.22
  4.5 0.1 rev.3
  4.6 1.1 multiply_convert_fusion
  5.8 0.1 broadcast_multiply_fusion.2
  5.9 13.6 %collective-permute-done = bf16[4,3,512,128]{3,2,1,0:T(8,128)(2,1)} collective-permute-done((bf16[4,3,512,128]{3,2,1,0:T(8,128)(2,1)}, bf16[4,3,512,128]{3,2,1,0:T(8,128)(2,1)}, u32[]{:S(2)}, u32[]{:S(2)}) %collective-permute-start) | collective-permute-done | bytes 1572896 | tf_op jit(solution)/shard_map/ppermute | solution.py:29
  19.6 3.4 %collective-permute-done.1 = bf16[4,3,512,128]{3,2,1,0:T(8,128)(2,1)} collective-permute-done((bf16[4,3,512,128]{3,2,1,0:T(8,128)(2,1)}, bf16[4,3,512,128]{3,2,1,0:T(8,128)(2,1)}, u32[]{:S(2)}, u32[]{:S(2)}) %collective-permute-start.1) | collective-permute-done | bytes 1572896 | tf_op jit(solution)/shard_map/ppermute | solution.py:30
  23.0 0.0 copy-done.1
  23.0 4.0 %convert_reduce_fusion = (f32[3,256,256]{2,1,0:T(8,128)S(1)}, bf16[4,3,256,256]{3,2,1,0:T(8,128)(2,1)S(1)}) fusion(s32[]{:T(128)S(6)} %select_n.39, s32[]{:T(128)S(6)} %select_n.41, bf16[4,3,512,128]{3,2,1,0:T(8,128)(2,1)} %collective-permute-done.1, bf16[4,3,512,128]{3,2,1,0:T(8,128)(2,1)S(1)} %copy-done.1, bf16[4,3,512,128]{3,2,1,0:T(8,128)(2,1)} %collective-permute-done), kind=kLoop, calls=%fused_computation.17 | loop fusion | flops 6094848 | bytes 7077896 | tf_op jit(solution)/shard_map/while/body/eval_jaxpr/reduce_sum | solution.py:103
  27.0 0.1 broadcast_multiply_fusion
  27.0 0.4 fusion.8
  27.5 8.5 %while.20 = (s32[]{:T(128)}, bf16[4,3,256,256]{2,3,1,0:T(8,128)(2,1)}, bf16[4,3,256,256]{2,3,1,0:T(8,128)(2,1)}, bf16[4,3,256,256]{3,2,1,0:T(8,128)(2,1)S(1)}, b...) while((s32[]{:T(128)}, bf16[4,3,256,256]{2,3,1,0:T(8,128)(2,1)}, ...), condition=%wide.region_2.3_spmd, body=%wide.region_1.2_spmd.sunk | while | flops 605159424 | bytes 10355281 | solution.py:105
  27.6 0.4 convolution_convert_fusion.2
  27.9 0.6 convolution_bitcast_fusion.2
  28.6 1.1 fusion.35
  29.7 0.4 convolution_convert_fusion.2
  30.0 0.6 convolution_bitcast_fusion.2
  30.7 1.1 fusion.35
  31.8 0.4 convolution_convert_fusion.2
  32.1 0.6 convolution_bitcast_fusion.2
  32.8 1.1 fusion.35
  33.9 0.4 convolution_convert_fusion.2
  34.2 0.6 convolution_bitcast_fusion.2
  34.9 1.1 fusion.35
  36.0 13.4 %concatenate.21 = bf16[12,16,16,16,16]{2,1,4,3,0:T(8,128)(2,1)} reshape(bf16[4,3,256,256]{2,3,1,0:T(8,128)(2,1)} %get-tuple-element.62) | data formatting | bytes 3145728 | tf_op jit(solution)/shard_map/while/body/eval_jaxpr/concatenate | solution.py:106
  49.3 0.0 copy-start
  49.3 16.9 %copy.33 = bf16[12,16,16,16,16]{4,2,3,1,0:T(8,128)(2,1)} copy(bf16[12,16,16,16,16]{2,1,4,3,0:T(8,128)(2,1)} %concatenate.21) | data formatting | bytes 3145728 | tf_op jit(solution)/shard_map/while/body/eval_jaxpr/concatenate | solution.py:106
  66.2 0.0 copy-done
  66.2 10.9 %concatenate.22 = bf16[12,16,16,16,16]{2,1,4,3,0:T(8,128)(2,1)} reshape(bf16[4,3,256,256]{2,3,1,0:T(8,128)(2,1)S(1)} %copy-done) | data formatting | bytes 3145728 | tf_op jit(solution)/shard_map/while/body/eval_jaxpr/concatenate | solution.py:106
  77.1 17.0 %copy.34 = bf16[12,16,16,16,16]{4,2,3,1,0:T(8,128)(2,1)} copy(bf16[12,16,16,16,16]{2,1,4,3,0:T(8,128)(2,1)} %concatenate.22) | data formatting | bytes 3145728 | tf_op jit(solution)/shard_map/while/body/eval_jaxpr/concatenate | solution.py:106
  94.1 28.8 %convert_bitcast_fusion = f32[16,16,24,16,16]{4,3,1,0,2:T(8,128)} fusion(bf16[12,16,16,16,16]{4,2,3,1,0:T(8,128)(2,1)} %copy.34, bf16[12,16,16,16,16]{4,2,3,1,0:T(8,128)(2,1)} %copy.33), kind=kLoop, calls=%fused_computation.12 | loop fusion | flops 3145728 | bytes 9437184 | tf_op jit(solution)/shard_map/convert_element_type | solution.py:61
  123.0 34.6 %reshape.406 = f32[1,256,2,4,3,256]{5,1,4,3,2,0:T(8,128)} reshape(f32[16,16,24,16,16]{4,3,1,0,2:T(8,128)} %convert_bitcast_fusion) | data formatting | bytes 12582912 | tf_op jit(solution)/shard_map/convert_element_type | solution.py:61
  157.6 3.5 %slice_bitcast_fusion.1 = (f32[1,256,4,3,256]{4,1,3,2,0:T(8,128)S(1)}, f32[1,256,4,3,256]{4,1,3,2,0:T(8,128)S(1)}) fusion(f32[1,256,2,4,3,256]{5,1,4,3,2,0:T(8,128)} %reshape.406), kind=kLoop, calls=%fused_computation.21 | loop fusion | bytes 12582912 | tf_op jit(solution)/shard_map/squeeze | solution.py:62
  161.1 0.9 add_reduce_fusion
  162.0 1.0 copy_dynamic-update-slice_fusion.4
  163.1 1.0 copy_dynamic-update-slice_fusion.3
  164.1 1.0 copy_dynamic-update-slice_fusion.2
  165.0 1.0 copy_dynamic-update-slice_fusion.1
  166.0 1.0 copy_dynamic-update-slice_fusion
  167.0 0.9 reshape_dynamic-update-slice_fusion
  167.9 0.0 copy-start.2
  167.9 20.7 %all-to-all-start = ((f32[1,256,6,256]{3,0,2,1:T(1,128)}), f32[1,256,6,256]{3,0,2,1:T(1,128)S(1)}, u32[]{:S(2)}, u32[]{:S(2)}) async-start(f32[1,256,6,256]{3,0,2,1:T(1,128)} %reshape_dynamic-update-slice_fusion), calls=%async_computation | async-start | bytes 3145728 | tf_op jit(solution)/shard_map/all_to_all | solution.py:118
  188.6 0.0 copy-done.2
  188.6 36.2 %all-to-all-done = f32[1,256,6,256]{3,0,2,1:T(1,128)S(1)} async-done(((f32[1,256,6,256]{3,0,2,1:T(1,128)}), f32[1,256,6,256]{3,0,2,1:T(1,128)S(1)}, u32[]{:S(2)}, u32[]{:S(2)}) %all-to-all-start) | async-done | bytes 1572896 | tf_op jit(solution)/shard_map/all_to_all | solution.py:118
  224.8 3.0 %reduce_sum.89 = f32[256,6]{1,0:T(8,128)S(1)} reduce(f32[1,256,6,256]{3,0,2,1:T(1,128)S(1)} %all-to-all-done, f32[]{:T(128)} %constant.101.clone.1), dimensions={0,3}, to_apply=%region_9.10 | reduce | flops 391680 | bytes 1579012 | tf_op jit(solution)/shard_map/reduce_sum | solution.py:119
  227.8 0.1 copy.42
  227.9 0.1 div.69
  228.0 0.1 copy.40
  228.2 0.3 multiply_add_fusion
  228.5 1.3 copy.43
  (20 shorter events, 0.4 us)
Async XLA Ops:
  0.0 23.0 %copy-start.1 = (bf16[4,3,512,128]{3,2,1,0:T(8,128)(2,1)S(1)}, bf16[4,3,512,128]{3,2,1,0:T(8,128)(2,1)}, u32[]{:S(2)}) copy-start(bf16[4,3,512,128]{3,2,1,0:T(8,128)(2,1)} %param.5) | copy-start | bytes 4718596
  0.0 19.5 %collective-permute-start = (bf16[4,3,512,128]{3,2,1,0:T(8,128)(2,1)}, bf16[4,3,512,128]{3,2,1,0:T(8,128)(2,1)}, u32[]{:S(2)}, u32[]{:S(2)}) collective-permute-start(bf16[4,3,512,128]{3,2,1,0:T(8,128)(2,1)} %param.5), channel_id=1, source_target_pairs={{0,1},{1,2},{2,3},{3,4},{4,5},{5,6},{6,7},{7,8},{8,9},{9,10},{10,1... | collective-permute-start | bytes 4718600 | tf_op jit(solution)/shard_map/ppermute | solution.py:29
  1.8 21.2 %collective-permute-start.1 = (bf16[4,3,512,128]{3,2,1,0:T(8,128)(2,1)}, bf16[4,3,512,128]{3,2,1,0:T(8,128)(2,1)}, u32[]{:S(2)}, u32[]{:S(2)}) collective-permute-start(bf16[4,3,512,128]{3,2,1,0:T(8,128)(2,1)} %param.5), channel_id=1, source_target_pairs={{1,0},{2,1},{3,2},{4,3},{5,4},{6,5},{7,6},{8,7},{9,8},{10,9},{11,1... | collective-permute-start | bytes 4718600 | tf_op jit(solution)/shard_map/ppermute | solution.py:30
  49.3 16.9 %copy-start = (bf16[4,3,256,256]{2,3,1,0:T(8,128)(2,1)S(1)}, bf16[4,3,256,256]{2,3,1,0:T(8,128)(2,1)}, u32[]{:S(2)}) copy-start(bf16[4,3,256,256]{2,3,1,0:T(8,128)(2,1)} %get-tuple-element.63) | copy-start | bytes 4718596
  167.9 20.7 %copy-start.2 = (s32[16,16]{1,0:T(8,128)S(1)}, s32[16,16]{1,0:T(8,128)}, u32[]{:S(2)}) copy-start(s32[16,16]{1,0:T(8,128)} %param.7) | copy-start | bytes 3076
  167.9 56.9 %all-to-all-start = ((f32[1,256,6,256]{3,0,2,1:T(1,128)}), f32[1,256,6,256]{3,0,2,1:T(1,128)S(1)}, u32[]{:S(2)}, u32[]{:S(2)}) async-start(f32[1,256,6,256]{3,0,2,1:T(1,128)} %reshape_dynamic-update-slice_fusion), calls=%async_computation | async-start | bytes 3145728 | tf_op jit(solution)/shard_map/all_to_all | solution.py:118
where the time goes:
time: 232 us; the launch traced here: 230 us
  local copies, waits for them, and re-layouts  105 us (45%)
  waiting for transfers between devices  53.2 us (23%)
  other arithmetic  43.4 us (19%)
  starting transfers between devices  22.5 us (10%)
  matrix products  3.95 us (2%)
    concatenate x4, local copies, waits for them, and re-layouts, one_tile(): jnp.concatenate([real_part.reshape(SPLITS * STOKES, TILE, TILE), imag_par...  58.2 us
    all_to_all x1, waiting for transfers between devices, body(): lax.all_to_all(local_cross, 'ra', split_axis=1, concat_axis=0, tiled=True)  36.2 us
    convert_element_type x1, local copies, waits for them, and re-layouts, cross_power(): values = stacked.astype(jnp.float32)  34.6 us
    convert_element_type x1, other arithmetic, cross_power(): values = stacked.astype(jnp.float32)  28.8 us
    all_to_all x1, starting transfers between devices, body(): lax.all_to_all(local_cross, 'ra', split_axis=1, concat_axis=0, tiled=True)  20.7 us
    ppermute x1, waiting for transfers between devices, with_halo(): before = lax.ppermute(last, axis, up)  13.6 us
    unnamed x11, local copies, waits for them, and re-layouts  4.88 us
  transfers between devices with their start and end apart: 3, of which 3 were waited for; matrix products, arithmetic and copies ran while one was open for 1% of the time, Pallas kernels for 0%

commit v1 on v0

--- a/solution.py
+++ b/solution.py
@@ -1,8 +1,11 @@
+import functools
 import math
 
 import jax
 import jax.numpy as jnp
 from jax import lax
+from jax.experimental import pallas as pl
+from jax.experimental.pallas import tpu as pltpu
 from jax.sharding import PartitionSpec as P
 
 SPLITS = 4
@@ -14,6 +17,10 @@
 TILE = 256
 FBS = 16
 FBLK = 256
+PAIRS = 6
+COMBOS = 3
+HALF = 128
+MESH = pl.DeviceIdType.MESH
 
 
 cov_pairs = ((0, 0), (1, 1), (2, 2), (0, 1), (0, 2), (1, 2))
@@ -71,7 +78,7 @@
     return jnp.stack(terms, axis=-2)
 
 
-def body(split_maps, tile_start, pattern):
+def plain_body(split_maps, tile_start, pattern):
     width = REACH * CBD * BPX
     window = with_halo(split_maps, (("ra", 3),), width)
     first_block = (lax.axis_index("ra") - REACH) * CBD
@@ -122,6 +129,324 @@
     return 0.5 * kept + 0.5 * level
 
 
+def combine(maps_ref, first_row, weight_y, weight_x, store):
+    first = jnp.broadcast_to(first_row, (BPX, HALF))
+    for block in range(TILE // BPX):
+        place = (block - first) & 3
+        up = jnp.where(place == 3, weight_y[1], 1.0)
+        weight = jnp.where(place == 0, weight_y[0], up) * (0.5 * weight_x)
+        upper = first <= block
+        for p in range(STOKES):
+            s = []
+            for split in range(SPLITS):
+                high = maps_ref[split, p, block * BPX : (block + 1) * BPX, :].astype(jnp.float32)
+                low = maps_ref[
+                    split, p, TILE + block * BPX : TILE + (block + 1) * BPX, :
+                ].astype(jnp.float32)
+                s.append(jnp.where(upper, high, low))
+            sum_a, sum_b = s[0] + s[1], s[2] + s[3]
+            dif_a, dif_b = s[0] - s[1], s[2] - s[3]
+            for k, value in enumerate((sum_a - sum_b, dif_a + dif_b, dif_a - dif_b)):
+                store(k, p * TILE + block * BPX, (value * weight).astype(jnp.bfloat16))
+
+
+def pick_x(offset_row, wx_ref, lanes):
+    rows = [wx_ref[m : m + 1, lanes] for m in range(3)]
+    return jnp.where(offset_row == 0, rows[0], jnp.where(offset_row == 1, rows[1], rows[2]))
+
+
+def power_kernel(
+    n,
+    info_ref,
+    maps_ref,
+    wy_ref,
+    wx_ref,
+    t1_ref,
+    t2_ref,
+    out_ref,
+    info_in,
+    halo_out,
+    halo_in,
+    own,
+    half_ref,
+    spec,
+    cross,
+    shuffle,
+    packed,
+    info_send,
+    info_recv,
+    halo_send,
+    halo_recv,
+    all_send,
+    all_recv,
+    local_sem,
+):
+    me = lax.axis_index("ra")
+    right, left = lax.rem(me + 1, n), lax.rem(me + n - 1, n)
+
+    barrier = pltpu.get_barrier_semaphore()
+
+    @pl.loop(1, n)
+    def _(step):
+        pl.semaphore_signal(
+            barrier, inc=1, device_id={"ra": lax.rem(me + step, n)}, device_id_type=MESH
+        )
+
+    pl.semaphore_wait(barrier, n - 1)
+
+    def info_copy(side):
+        return pltpu.make_async_remote_copy(
+            src_ref=info_ref,
+            dst_ref=info_in.at[side],
+            send_sem=info_send.at[side],
+            recv_sem=info_recv.at[side],
+            device_id={"ra": (right, left)[side]},
+            device_id_type=MESH,
+        )
+
+    def halo_copy(side, k):
+        return pltpu.make_async_remote_copy(
+            src_ref=halo_out.at[side, k],
+            dst_ref=halo_in.at[side, k],
+            send_sem=halo_send.at[side, k],
+            recv_sem=halo_recv.at[side, k],
+            device_id={"ra": (right, left)[side]},
+            device_id_type=MESH,
+        )
+
+    def power_copy(to, source):
+        return pltpu.make_async_remote_copy(
+            src_ref=packed.at[to],
+            dst_ref=out_ref.at[source],
+            send_sem=all_send.at[to],
+            recv_sem=all_recv.at[source],
+            device_id={"ra": to},
+            device_id_type=MESH,
+        )
+
+    for side in range(2):
+        info_copy(side).start()
+
+    lane = lax.broadcasted_iota(jnp.int32, (1, HALF), 1)
+
+    def store_own(k, row, value):
+        own[k, row : row + BPX, :] = value
+
+    combine(
+        maps_ref,
+        info_ref[0:1, :],
+        wy_ref,
+        pick_x(info_ref[1:2, :], wx_ref, slice(HALF, TILE)),
+        store_own,
+    )
+
+    for side in range(2):
+        info_copy(1 - side).wait_recv()
+        offset_row = info_in[1 - side, 1:2, :]
+        weight_x = pick_x(offset_row, wx_ref, slice(0, HALF))
+        inside = (lane >= BPX * offset_row) if side == 0 else (lane < BPX * offset_row)
+
+        def store_halo(k, row, value):
+            halo_out[side, k, row : row + BPX, :] = value
+
+        combine(
+            maps_ref,
+            info_in[1 - side, 0:1, :],
+            wy_ref,
+            jnp.where(inside, weight_x, 0.0),
+            store_halo,
+        )
+        for k in range(COMBOS):
+            halo_copy(side, k).start()
+
+    cross[...] = jnp.zeros_like(cross)
+
+    @pl.loop(0, COMBOS)
+    def _(k):
+        for side in range(2):
+            halo_copy(side, k).wait_recv()
+        for p in range(STOKES):
+            rows = slice(p * TILE, (p + 1) * TILE)
+            outer = halo_in[0, k, rows, :] + halo_in[1, k, rows, :]
+            pixels = jnp.concatenate([outer, own[k, rows, :]], axis=1)
+            half_ref[0:TILE, :] = jnp.dot(
+                pixels, t1_ref[:, 0:TILE], preferred_element_type=jnp.float32
+            ).astype(jnp.bfloat16)
+            half_ref[TILE : 2 * TILE, :] = jnp.dot(
+                pixels, t1_ref[:, TILE : 2 * TILE], preferred_element_type=jnp.float32
+            ).astype(jnp.bfloat16)
+            spec[p] = jnp.dot(t2_ref[...], half_ref[...], preferred_element_type=jnp.float32)
+
+        @pl.loop(0, TILE // 16)
+        def _(step):
+            start = pl.multiple_of(step * 16, 16)
+            real = [spec[p, pl.ds(start, 16), :] for p in range(STOKES)]
+            imag = [spec[p, pl.ds(start + TILE, 16), :] for p in range(STOKES)]
+            for c, (a, b) in enumerate(cov_pairs):
+                cross[c, pl.ds(start, 16), :] += real[a] * real[b] + imag[a] * imag[b]
+
+    my_half = me // 8
+
+    @pl.loop(0, 2)
+    def _(turn):
+        part = lax.rem(my_half + 1 + turn, 2)
+        base = part * HALF
+
+        @pl.loop(0, PAIRS)
+        def _(c):
+            for ih in range(2):
+                for vh in range(2):
+                    x = [
+                        cross[
+                            c,
+                            pl.ds(pl.multiple_of(base + (8 * ih + i) * 8, 8), 8),
+                            vh * HALF : (vh + 1) * HALF,
+                        ]
+                        for i in range(8)
+                    ]
+                    for bit in range(3):
+                        shift = FBS << bit
+                        low = ((lane >> (4 + bit)) & 1) == 0
+                        y = list(x)
+                        for i in range(8):
+                            if not i >> bit & 1:
+                                j = i | 1 << bit
+                                y[i] = jnp.where(low, x[i], pltpu.roll(x[j], shift, 1))
+                                y[j] = jnp.where(low, pltpu.roll(x[i], HALF - shift, 1), x[j])
+                        x = y
+                    for v in range(8):
+                        shuffle[ih, pl.ds((8 * vh + v) * PAIRS + c, 8, stride=FBN * PAIRS), :] = x[v]
+
+        @pl.loop(0, 8)
+        def _(step):
+            u = lax.rem(me + step, 8)
+            to = part * 8 + u
+            rows = pl.ds(pl.multiple_of(u * FBN * PAIRS, 8), FBN * PAIRS)
+            for ih in range(2):
+                packed[to, :, ih * HALF : (ih + 1) * HALF] = (
+                    shuffle[ih, rows, :] * 0.25
+                ).astype(jnp.bfloat16)
+
+            @pl.when(to != me)
+            def _():
+                power_copy(to, me).start()
+
+            @pl.when(to == me)
+            def _():
+                pltpu.make_async_copy(packed.at[me], out_ref.at[me], local_sem).start()
+
+    for side in range(2):
+        info_copy(side).wait_send()
+        for k in range(COMBOS):
+            halo_copy(side, k).wait_send()
+    pltpu.make_async_copy(packed.at[me], out_ref.at[me], local_sem).wait()
+
+    @pl.loop(1, n)
+    def _(step):
+        other = lax.rem(me + step, n)
+        power_copy(other, other).wait_recv()
+        power_copy(other, other).wait_send()
+
+
+def finish_kernel(pattern_ref, ones_ref, power_ref, out_ref, wide, means):
+    tiles, rows = power_ref.shape[0], power_ref.shape[1]
+    level = jnp.zeros((rows, HALF), jnp.float32)
+    for t in range(tiles):
+        values = power_ref[t]
+        mean = jnp.dot(values, ones_ref[...], preferred_element_type=jnp.float32)
+        means[t] = mean
+        level = level + mean
+        wide[t] = values.astype(jnp.float32)
+    means[tiles] = level * (0.5 / tiles)
+    blocks = rows // PAIRS
+
+    @pl.loop(0, tiles)
+    def _(t):
+        for v in range(blocks):
+            own = slice(v * PAIRS, (v + 1) * PAIRS)
+            keep = pattern_ref[t, v] == 1
+            mean, base = means[t, own, :], means[tiles, own, :]
+            for ih in range(2):
+                lanes = slice(ih * HALF, (ih + 1) * HALF)
+                kept = jnp.where(keep, wide[t, own, lanes], mean)
+                out_ref[t, v, :, lanes] = 0.5 * kept + base
+
+
+def kernel_body(split_maps, tile_start, pattern):
+    n = lax.axis_size("ra")
+    offset = (tile_start[0, 1] - (lax.axis_index("ra") - REACH) * CBD) % (CBD * n)
+    row = lax.broadcasted_iota(jnp.int32, (8, HALF), 0)
+    info = jnp.where(row == 0, tile_start[0, 0], offset).astype(jnp.int32)
+    cosine, sine = fourier_tables(TILE)
+    section_one = jnp.concatenate([cosine, sine], axis=1)
+    order = jnp.asarray(
+        [16 * (8 * h + u) + i for h in range(2) for i in range(16) for u in range(8)], jnp.int32
+    )
+    order_cos, order_sin = cosine[order], sine[order]
+    section_two = jnp.concatenate(
+        [
+            jnp.concatenate([order_cos, -order_sin], axis=1),
+            jnp.concatenate([order_sin, order_cos], axis=1),
+        ],
+        axis=0,
+    )
+    edge = TILE // 8
+    counter = jnp.arange(TILE, dtype=jnp.float32)
+    rising = jnp.where(counter < edge, jnp.sin(math.pi * (counter + 0.5) / (2 * edge)) ** 2, 1.0)
+    line = rising * rising[::-1]
+    weight_y = jnp.broadcast_to(
+        jnp.stack([line[:BPX], line[TILE - BPX :]])[:, :, None], (2, BPX, HALF)
+    )
+    weight_x = jnp.stack([jnp.roll(line, BPX * (m % 4)) for m in range(8)])
+    rows = FBN * PAIRS
+    vmem = pl.BlockSpec(memory_space=pltpu.VMEM)
+    power = pl.pallas_call(
+        functools.partial(power_kernel, n),
+        out_shape=jax.ShapeDtypeStruct((n, rows, TILE), jnp.bfloat16),
+        in_specs=[vmem] * 6,
+        out_specs=pl.BlockSpec(memory_space=pl.ANY),
+        scratch_shapes=[
+            pltpu.VMEM((2, 8, HALF), jnp.int32),
+            pltpu.VMEM((2, COMBOS, STOKES * TILE, HALF), jnp.bfloat16),
+            pltpu.VMEM((2, COMBOS, STOKES * TILE, HALF), jnp.bfloat16),
+            pltpu.VMEM((COMBOS, STOKES * TILE, HALF), jnp.bfloat16),
+            pltpu.VMEM((2 * TILE, TILE), jnp.bfloat16),
+            pltpu.VMEM((STOKES, 2 * TILE, TILE), jnp.float32),
+            pltpu.VMEM((PAIRS, TILE, TILE), jnp.float32),
+            pltpu.VMEM((2, 8 * rows, HALF), jnp.float32),
+            pltpu.VMEM((n, rows, TILE), jnp.bfloat16),
+            pltpu.SemaphoreType.DMA((2,)),
+            pltpu.SemaphoreType.DMA((2,)),
+            pltpu.SemaphoreType.DMA((2, COMBOS)),
+            pltpu.SemaphoreType.DMA((2, COMBOS)),
+            pltpu.SemaphoreType.DMA((n,)),
+            pltpu.SemaphoreType.DMA((n,)),
+            pltpu.SemaphoreType.DMA,
+        ],
+        compiler_params=pltpu.CompilerParams(
+            collective_id=0, has_side_effects=True, vmem_limit_bytes=48 * 2**20
+        ),
+    )(info, split_maps, weight_y, weight_x, section_one, section_two)
+    ones = jnp.full((TILE, HALF), 1.0 / TILE, jnp.bfloat16)
+    return pl.pallas_call(
+        finish_kernel,
+        out_shape=jax.ShapeDtypeStruct((n, FBN, PAIRS, TILE), jnp.float32),
+        in_specs=[pl.BlockSpec(memory_space=pltpu.SMEM), vmem, vmem],
+        out_specs=vmem,
+        scratch_shapes=[
+            pltpu.VMEM((n, rows, TILE), jnp.float32),
+            pltpu.VMEM((n + 1, rows, HALF), jnp.float32),
+        ],
+        compiler_params=pltpu.CompilerParams(vmem_limit_bytes=32 * 2**20),
+    )(pattern, ones, power)
+
+
+def body(split_maps, tile_start, pattern):
+    if lax.axis_size("ra") == FBN:
+        return kernel_body(split_maps, tile_start, pattern)
+    return plain_body(split_maps, tile_start, pattern)
+
+
 def solution(mesh):
     placed = (P(None, None, "grp", "ra"), P(("grp", "ra"), None), P("grp", "ra"))
     return jax.shard_map(

time: 232 us -> 52.6 us (0.23)
  the two profiles are of different devices: /device:TPU:15 before, /device:TPU:0 now
where the time goes in v1:
time: 52.6 us; the launch traced here: 52.4 us
  Pallas kernels  43.2 us (82%)
  local copies, waits for them, and re-layouts  5.83 us (11%)
  other arithmetic  2.72 us (5%)
  between operations  0.69 us (1%)
    pallas_call x1, Pallas kernels, kernel_body(): pl.pallas_call(functools.partial(power_kernel, n), out_shape=jax.ShapeDty...  41.4 us
    gather x2, local copies, waits for them, and re-layouts, kernel_body(): order_cos, order_sin = (cosine[order], sine[order])  2.3 us
    pallas_call x1, Pallas kernels, kernel_body(): pl.pallas_call(finish_kernel, out_shape=jax.ShapeDtypeStruct((n, FBN, PAI...  1.73 us
    pallas_call x1, local copies, waits for them, and re-layouts, kernel_body(): pl.pallas_call(finish_kernel, out_shape=jax.ShapeDtypeStruct((n, FBN, PAI...  1.65 us
    slice x1, local copies, waits for them, and re-layouts, kernel_body(): info = jnp.where(row == 0, tile_start[0, 0], offset).astype(jnp.int32)  1.31 us
    convert_element_type x1, other arithmetic, fourier_tables(): (jnp.sin(angle) * factor).astype(jnp.bfloat16)  1.11 us

profile of v1, /device:TPU:0, one launch (start us, length us, event | category | flops | bytes accessed | tf_op | source)
XLA Modules:
  0.0 52.4 jit_solution(17654293386015713932)
XLA Ops:
  0.0 0.1 rev.3
  0.2 1.3 %fusion.13 = (s32[1,1]{1,0:T(1,128)}, s32[1,1]{1,0:T(1,128)}) fusion(s32[1,2]{1,0:T(1,128)} %param.5), kind=kLoop, calls=%fused_computation.32 | loop fusion | bytes 16 | tf_op jit(solution)/shard_map/slice | solution.py:379
  2.1 0.7 %compare_select_fusion.1 = s32[8]{0:T(128)S(1)} fusion(s32[]{:T(128)S(6)} %select_n.33, s32[]{:T(128)} %bitcast), kind=kLoop, calls=%fused_computation.17 | loop fusion | flops 16 | bytes 40 | tf_op jit(solution)/shard_map/jit(_where)/select_n | solution.py:379
  2.8 0.1 fusion.11
  2.9 0.1 fusion.10
  2.9 0.1 pad_maximum_fusion.2
  3.0 0.1 iota.19.info_ref
  3.1 0.7 %pad_clamp_fusion = s32[1024]{0:T(1024)S(1)} fusion(s32[256]{0:T(256)} %constant.64), kind=kLoop, calls=%fused_computation.15 | loop fusion | flops 1024 | bytes 5120 | tf_op jit(solution)/shard_map/gather | solution.py:385
  3.8 0.1 broadcast_in_dim.31.wy_ref
  3.9 1.1 %multiply_convert_fusion = (bf16[256,256]{1,0:T(8,128)(2,1)S(1)}, bf16[256,256]{1,0:T(8,128)(2,1)S(1)}) fusion(), kind=kLoop, calls=%fused_computation.10 | loop fusion | flops 1179648 | bytes 262144 | tf_op jit(solution)/shard_map/convert_element_type | solution.py:49
  5.0 1.2 %gather_fusion.1 = bf16[256,256]{1,0:T(8,128)(2,1)S(1)} fusion(bf16[256,256]{1,0:T(8,128)(2,1)S(1)} %get-tuple-element.17, s32[1024]{0:T(1024)S(1)} %pad_clamp_fusion), kind=kCustom, calls=%fused_computation.1 | custom fusion | bytes 263168 | tf_op jit(solution)/shard_map/gather | solution.py:385
  6.1 0.0 copy-start
  6.1 1.2 %gather_fusion = bf16[256,256]{1,0:T(8,128)(2,1)S(1)} fusion(bf16[256,256]{1,0:T(8,128)(2,1)S(1)} %get-tuple-element.18, s32[1024]{0:T(1024)S(1)} %pad_clamp_fusion), kind=kCustom, calls=%fused_computation | custom fusion | bytes 263168 | tf_op jit(solution)/shard_map/gather | solution.py:385
  7.4 0.1 copy-done
  7.5 0.0 copy-start.1
  7.5 41.4 %shard_map.46.power_ref = bf16[16,96,256]{2,1,0:T(8,128)(2,1)S(1)} custom-call(s32[8,128]{1,0:T(8,128)S(1)} %iota.19.info_ref, bf16[4,3,512,128]{3,2,1,0:T(8,128)(2,1)S(1)} %copy-done, f32[2,64,128]{2,1,0:T(8,128)S(1)} %broadcast_in_dim.31.wy_ref, f32[8,256]{1,0:T(8,128)S(1)} %stack.35.wx_ref, bf16[256,512]{1,0:T(8,128)(2,1)S(1)} %pad_maximum_fusion.t1_ref, ...), custom_call_target="tpu_custom_call" | custom-call | tf_op jit(solution)/shard_map/pallas_call | solution.py:403
  49.0 0.0 copy-done.1
  49.0 1.7 %shard_map.47 = f32[16,16,6,256]{3,2,1,0:T(8,128)S(1)} custom-call(s32[16,16]{1,0:T(8,128)S(1)} %copy-done.1, bf16[256,128]{1,0:T(8,128)(2,1)S(1)} %broadcast_in_dim.27.ones_ref, bf16[16,96,256]{2,1,0:T(8,128)(2,1)S(1)} %shard_map.46.power_ref), custom_call_target="tpu_custom_call" | custom-call | tf_op jit(solution)/shard_map/pallas_call | solution.py:431
  50.8 1.6 %copy.5 = f32[16,16,6,256]{3,1,2,0:T(8,128)} copy(f32[16,16,6,256]{3,2,1,0:T(8,128)S(1)} %shard_map.47) | data formatting | bytes 3145728 | tf_op jit(solution)/shard_map/pallas_call | solution.py:431
  (10 shorter events, 0.2 us)
Async XLA Ops:
  6.1 1.4 %copy-start = (bf16[4,3,512,128]{3,2,1,0:T(8,128)(2,1)S(1)}, bf16[4,3,512,128]{3,2,1,0:T(8,128)(2,1)}, u32[]{:S(2)}) copy-start(bf16[4,3,512,128]{3,2,1,0:T(8,128)(2,1)} %maps_ref.1) | copy-start | bytes 4718596
  7.5 41.5 %copy-start.1 = (s32[16,16]{1,0:T(8,128)S(1)}, s32[16,16]{1,0:T(8,128)}, u32[]{:S(2)}) copy-start(s32[16,16]{1,0:T(8,128)} %pattern_ref.1) | copy-start | bytes 3076

commit v2 on v0

--- a/solution.py
+++ b/solution.py
@@ -1,8 +1,13 @@
+import functools
 import math
 
 import jax
 import jax.numpy as jnp
+import ml_dtypes
+import numpy as np
 from jax import lax
+from jax.experimental import pallas as pl
+from jax.experimental.pallas import tpu as pltpu
 from jax.sharding import PartitionSpec as P
 
 SPLITS = 4
@@ -14,6 +19,10 @@
 TILE = 256
 FBS = 16
 FBLK = 256
+PAIRS = 6
+COMBOS = 3
+HALF = 128
+MESH = pl.DeviceIdType.MESH
 
 
 cov_pairs = ((0, 0), (1, 1), (2, 2), (0, 1), (0, 2), (1, 2))
@@ -71,7 +80,7 @@
     return jnp.stack(terms, axis=-2)
 
 
-def body(split_maps, tile_start, pattern):
+def plain_body(split_maps, tile_start, pattern):
     width = REACH * CBD * BPX
     window = with_halo(split_maps, (("ra", 3),), width)
     first_block = (lax.axis_index("ra") - REACH) * CBD
@@ -122,6 +131,382 @@
     return 0.5 * kept + 0.5 * level
 
 
+arrival_pairs = ((0, 0), (1, 1), (0, 1), (2, 2), (0, 2), (1, 2))
+places = tuple(cov_pairs.index(pair) for pair in arrival_pairs)
+pieces = ((0, 1), (1, 2), (3, 3))
+
+
+def combine(maps_ref, p, first_row, weight_y, weight_x, target):
+    first = jnp.broadcast_to(first_row, (BPX, HALF))
+    for block in range(TILE // BPX):
+        place = (block - first) & 3
+        up = jnp.where(place == 3, weight_y[1], 1.0)
+        weight = jnp.where(place == 0, weight_y[0], up) * (0.5 * weight_x)
+        upper = first <= block
+        s = []
+        for split in range(SPLITS):
+            high = maps_ref[split, p, block * BPX : (block + 1) * BPX, :].astype(jnp.float32)
+            low = maps_ref[
+                split, p, TILE + block * BPX : TILE + (block + 1) * BPX, :
+            ].astype(jnp.float32)
+            s.append(jnp.where(upper, high, low))
+        sum_a, sum_b = s[0] + s[1], s[2] + s[3]
+        dif_a, dif_b = s[0] - s[1], s[2] - s[3]
+        for k, value in enumerate((sum_a - sum_b, dif_a + dif_b, dif_a - dif_b)):
+            row = k * TILE + block * BPX
+            target[row : row + BPX, :] = (value * weight).astype(jnp.bfloat16)
+
+
+def pick_x(offset_row, wx_ref, lanes):
+    rows = [wx_ref[m : m + 1, lanes] for m in range(3)]
+    return jnp.where(offset_row == 0, rows[0], jnp.where(offset_row == 1, rows[1], rows[2]))
+
+
+def power_kernel(
+    n,
+    corner_ref,
+    maps_in,
+    wy_in,
+    wx_in,
+    t1_in,
+    t2_in,
+    out_ref,
+    maps_ref,
+    wy_ref,
+    wx_ref,
+    t1_ref,
+    t2_ref,
+    info_ref,
+    info_in,
+    halo_out,
+    halo_in,
+    own,
+    half_ref,
+    spec,
+    cross,
+    shuffle,
+    packed,
+    info_send,
+    info_recv,
+    halo_send,
+    halo_recv,
+    all_send,
+    all_recv,
+    local_sem,
+    load_sem,
+):
+    me = lax.axis_index("ra")
+    right, left = lax.rem(me + 1, n), lax.rem(me + n - 1, n)
+
+    loads = [
+        pltpu.make_async_copy(source, target, load_sem.at[i])
+        for i, (source, target) in enumerate(
+            (
+                (maps_in, maps_ref),
+                (wy_in, wy_ref),
+                (wx_in, wx_ref),
+                (t1_in, t1_ref),
+                (t2_in, t2_ref),
+            )
+        )
+    ]
+    for load in loads:
+        load.start()
+    row = lax.broadcasted_iota(jnp.int32, (8, HALF), 0)
+    offset = lax.rem(corner_ref[0, 1] - (me - REACH) * CBD + CBD * n, CBD * n)
+    info_ref[...] = jnp.where(row == 0, corner_ref[0, 0], offset)
+
+    barrier = pltpu.get_barrier_semaphore()
+
+    @pl.loop(1, n)
+    def _(step):
+        pl.semaphore_signal(
+            barrier, inc=1, device_id={"ra": lax.rem(me + step, n)}, device_id_type=MESH
+        )
+
+    pl.semaphore_wait(barrier, n - 1)
+
+    def info_copy(side):
+        return pltpu.make_async_remote_copy(
+            src_ref=info_ref,
+            dst_ref=info_in.at[side],
+            send_sem=info_send.at[side],
+            recv_sem=info_recv.at[side],
+            device_id={"ra": (right, left)[side]},
+            device_id_type=MESH,
+        )
+
+    def halo_copy(side, p):
+        return pltpu.make_async_remote_copy(
+            src_ref=halo_out.at[side, p],
+            dst_ref=halo_in.at[side, p],
+            send_sem=halo_send.at[side, p],
+            recv_sem=halo_recv.at[side, p],
+            device_id={"ra": (right, left)[side]},
+            device_id_type=MESH,
+        )
+
+    def power_copy(piece, to, source):
+        first, count = pieces[piece]
+        rows = pl.ds(first * FBN, count * FBN)
+        return pltpu.make_async_remote_copy(
+            src_ref=packed.at[to, rows],
+            dst_ref=out_ref.at[source, rows],
+            send_sem=all_send.at[piece, to],
+            recv_sem=all_recv.at[piece, source],
+            device_id={"ra": to},
+            device_id_type=MESH,
+        )
+
+    for side in range(2):
+        info_copy(side).start()
+
+    lane = lax.broadcasted_iota(jnp.int32, (1, HALF), 1)
+    for load in loads[:3]:
+        load.wait()
+
+    own_x = pick_x(info_ref[1:2, :], wx_ref, slice(HALF, TILE))
+    for p in range(STOKES):
+        combine(maps_ref, p, info_ref[0:1, :], wy_ref, own_x, own.at[p])
+
+    halo_x = []
+    for side in range(2):
+        info_copy(1 - side).wait_recv()
+        offset_row = info_in[1 - side, 1:2, :]
+        inside = (lane >= BPX * offset_row) if side == 0 else (lane < BPX * offset_row)
+        halo_x.append(jnp.where(inside, pick_x(offset_row, wx_ref, slice(0, HALF)), 0.0))
+    for p in range(STOKES):
+        for side in range(2):
+            combine(
+                maps_ref,
+                p,
+                info_in[1 - side, 0:1, :],
+                wy_ref,
+                halo_x[side],
+                halo_out.at[side, p],
+            )
+            halo_copy(side, p).start()
+    for load in loads[3:]:
+        load.wait()
+
+    my_half = me // 8
+    for p in range(STOKES):
+        for side in range(2):
+            halo_copy(side, p).wait_recv()
+
+        @pl.loop(0, COMBOS)
+        def _(k):
+            rows = pl.ds(pl.multiple_of(k * TILE, TILE), TILE)
+            outer = halo_in[0, p, rows, :] + halo_in[1, p, rows, :]
+            pixels = jnp.concatenate([outer, own[p, rows, :]], axis=1)
+            half_ref[0:TILE, :] = jnp.dot(
+                pixels, t1_ref[:, 0:TILE], preferred_element_type=jnp.float32
+            ).astype(jnp.bfloat16)
+            half_ref[TILE : 2 * TILE, :] = jnp.dot(
+                pixels, t1_ref[:, TILE : 2 * TILE], preferred_element_type=jnp.float32
+            ).astype(jnp.bfloat16)
+            spec[p, k] = jnp.dot(t2_ref[...], half_ref[...], preferred_element_type=jnp.float32)
+
+        first, count = pieces[p]
+
+        @pl.loop(0, TILE // 8)
+        def _(step):
+            start = pl.multiple_of(step * 8, 8)
+            total = [None] * count
+            for k in range(COMBOS):
+                real = [spec[q, k, pl.ds(start, 8), :] for q in range(p + 1)]
+                imag = [spec[q, k, pl.ds(start + TILE, 8), :] for q in range(p + 1)]
+                for i, (a, b) in enumerate(arrival_pairs[first : first + count]):
+                    term = real[a] * real[b] + imag[a] * imag[b]
+                    total[i] = term if k == 0 else total[i] + term
+            for i in range(count):
+                cross[first + i, pl.ds(start, 8), :] = 0.25 * total[i]
+
+        @pl.loop(0, 2)
+        def _(turn):
+            part = lax.rem(my_half + 1 + turn, 2)
+            base = part * HALF
+
+            @pl.loop(first, first + count)
+            def _(c):
+                for ih in range(2):
+                    for vh in range(2):
+                        x = [
+                            cross[
+                                c,
+                                pl.ds(pl.multiple_of(base + (8 * ih + i) * 8, 8), 8),
+                                vh * HALF : (vh + 1) * HALF,
+                            ]
+                            for i in range(8)
+                        ]
+                        for bit in range(3):
+                            shift = FBS << bit
+                            low = ((lane >> (4 + bit)) & 1) == 0
+                            y = list(x)
+                            for i in range(8):
+                                if not i >> bit & 1:
+                                    j = i | 1 << bit
+                                    y[i] = jnp.where(low, x[i], pltpu.roll(x[j], shift, 1))
+                                    y[j] = jnp.where(low, pltpu.roll(x[i], HALF - shift, 1), x[j])
+                            x = y
+                        for v in range(8):
+                            rows = pl.ds(c * FBN + 8 * vh + v, 8, stride=FBN * PAIRS)
+                            shuffle[ih, rows, :] = x[v]
+
+            @pl.loop(0, 8)
+            def _(step):
+                u = lax.rem(me + step, 8)
+                to = part * 8 + u
+                rows = pl.ds(pl.multiple_of(u * FBN * PAIRS + first * FBN, 8), count * FBN)
+                for ih in range(2):
+                    packed[
+                        to, first * FBN : (first + count) * FBN, ih * HALF : (ih + 1) * HALF
+                    ] = shuffle[ih, rows, :].astype(jnp.bfloat16)
+
+                @pl.when(to != me)
+                def _():
+                    power_copy(p, to, me).start()
+
+    mine = pltpu.make_async_copy(packed.at[me], out_ref.at[me], local_sem)
+    mine.start()
+    for side in range(2):
+        info_copy(side).wait_send()
+        for p in range(STOKES):
+            halo_copy(side, p).wait_send()
+
+    for p in range(STOKES):
+
+        @pl.loop(1, n)
+        def _(step):
+            other = lax.rem(me + step, n)
+            power_copy(p, other, other).wait_recv()
+            power_copy(p, other, other).wait_send()
+
+    mine.wait()
+
+
+def finish_kernel(pattern_in, power_in, out_ref, pattern_ref, power_ref, means, load_sem):
+    tiles, rows = power_ref.shape[:2]
+    step, count = pl.program_id(0), out_ref.shape[0]
+
+    @pl.when(step == 0)
+    def _():
+        loads = [
+            pltpu.make_async_copy(power_in, power_ref, load_sem.at[0]),
+            pltpu.make_async_copy(pattern_in, pattern_ref, load_sem.at[1]),
+        ]
+        for load in loads:
+            load.start()
+        for load in loads:
+            load.wait()
+        ones = jnp.full((TILE, HALF), 1.0 / TILE, jnp.bfloat16)
+        level = jnp.zeros((rows, HALF), jnp.float32)
+        for t in range(tiles):
+            mean = jnp.dot(power_ref[t], ones, preferred_element_type=jnp.float32)
+            means[t] = mean
+            level = level + mean
+        means[tiles] = level * (0.5 / tiles)
+
+    square = (FBN, FBN)
+    diagonal = lax.broadcasted_iota(jnp.int32, square, 0) == lax.broadcasted_iota(
+        jnp.int32, square, 1
+    )
+    for i in range(count):
+        t = step * count + i
+        chosen = jnp.where(diagonal & (pattern_ref[pl.ds(t, 1), :] == 1), 1.0, 0.0)
+        keep = jnp.broadcast_to(jnp.sum(chosen, axis=1, keepdims=True), (FBN, HALF)) > 0.5
+        for c in range(PAIRS):
+            own = slice(c * FBN, (c + 1) * FBN)
+            mean, base = means[t, own, :], means[tiles, own, :]
+            for ih in range(2):
+                lanes = slice(ih * HALF, (ih + 1) * HALF)
+                kept = jnp.where(keep, power_ref[t, own, lanes].astype(jnp.float32), mean)
+                out_ref[i, places[c], :, lanes] = 0.5 * kept + base
+
+
+def constant_tables():
+    counter = np.arange(TILE)
+    angle = 2.0 * math.pi / TILE * (counter[:, None] * counter[None, :] % TILE)
+    cosine, sine = np.cos(angle) / math.sqrt(TILE), np.sin(angle) / math.sqrt(TILE)
+    section_one = np.concatenate([cosine, sine], axis=1)
+    order = counter.reshape(2, 8, FBS).transpose(0, 2, 1).reshape(-1)
+    cosine, sine = cosine[order], sine[order]
+    section_two = np.block([[cosine, -sine], [sine, cosine]])
+    edge = TILE // 8
+    rising = np.where(counter < edge, np.sin(math.pi * (counter + 0.5) / (2 * edge)) ** 2, 1.0)
+    line = (rising * rising[::-1]).astype(np.float32)
+    weight_y = np.stack([line[:BPX], line[TILE - BPX :]])
+    weight_y = np.ascontiguousarray(np.broadcast_to(weight_y[:, :, None], (2, BPX, HALF)))
+    weight_x = np.stack([np.roll(line, BPX * (m % 4)) for m in range(8)])
+    low = ml_dtypes.bfloat16
+    single = lambda table: table.astype(np.float32).astype(low)
+    return weight_y, weight_x, single(section_one), single(section_two)
+
+
+def kernel_body(split_maps, tile_start, pattern):
+    n = lax.axis_size("ra")
+    weight_y, weight_x, section_one, section_two = map(jnp.asarray, constant_tables())
+    rows = FBN * PAIRS
+    smem = pl.BlockSpec(memory_space=pltpu.SMEM)
+    hbm = pl.BlockSpec(memory_space=pltpu.HBM)
+    power = pl.pallas_call(
+        functools.partial(power_kernel, n),
+        out_shape=jax.ShapeDtypeStruct((n, rows, TILE), jnp.bfloat16),
+        in_specs=[smem] + [hbm] * 5,
+        out_specs=pl.BlockSpec(memory_space=pl.ANY),
+        scratch_shapes=[
+            pltpu.VMEM(split_maps.shape, jnp.bfloat16),
+            pltpu.VMEM(weight_y.shape, jnp.float32),
+            pltpu.VMEM(weight_x.shape, jnp.float32),
+            pltpu.VMEM(section_one.shape, jnp.bfloat16),
+            pltpu.VMEM(section_two.shape, jnp.bfloat16),
+            pltpu.VMEM((8, HALF), jnp.int32),
+            pltpu.VMEM((2, 8, HALF), jnp.int32),
+            pltpu.VMEM((2, STOKES, COMBOS * TILE, HALF), jnp.bfloat16),
+            pltpu.VMEM((2, STOKES, COMBOS * TILE, HALF), jnp.bfloat16),
+            pltpu.VMEM((STOKES, COMBOS * TILE, HALF), jnp.bfloat16),
+            pltpu.VMEM((2 * TILE, TILE), jnp.bfloat16),
+            pltpu.VMEM((STOKES, COMBOS, 2 * TILE, TILE), jnp.float32),
+            pltpu.VMEM((PAIRS, TILE, TILE), jnp.float32),
+            pltpu.VMEM((2, 8 * rows, HALF), jnp.float32),
+            pltpu.VMEM((n, rows, TILE), jnp.bfloat16),
+            pltpu.SemaphoreType.DMA((2,)),
+            pltpu.SemaphoreType.DMA((2,)),
+            pltpu.SemaphoreType.DMA((2, STOKES)),
+            pltpu.SemaphoreType.DMA((2, STOKES)),
+            pltpu.SemaphoreType.DMA((len(pieces), n)),
+            pltpu.SemaphoreType.DMA((len(pieces), n)),
+            pltpu.SemaphoreType.DMA,
+            pltpu.SemaphoreType.DMA((5,)),
+        ],
+        compiler_params=pltpu.CompilerParams(
+            collective_id=0, has_side_effects=True, vmem_limit_bytes=64 * 2**20 - 2**16
+        ),
+    )(tile_start, split_maps, weight_y, weight_x, section_one, section_two)
+    count = n // 4
+    result = pl.pallas_call(
+        finish_kernel,
+        out_shape=jax.ShapeDtypeStruct((n, PAIRS, FBN, TILE), jnp.float32),
+        grid=(n // count,),
+        in_specs=[hbm, hbm],
+        out_specs=pl.BlockSpec((count, PAIRS, FBN, TILE), lambda step: (step, 0, 0, 0)),
+        scratch_shapes=[
+            pltpu.VMEM(pattern.shape, jnp.int32),
+            pltpu.VMEM(power.shape, jnp.bfloat16),
+            pltpu.VMEM((n + 1, rows, HALF), jnp.float32),
+            pltpu.SemaphoreType.DMA((2,)),
+        ],
+        compiler_params=pltpu.CompilerParams(vmem_limit_bytes=64 * 2**20 - 2**16),
+    )(pattern, power)
+    return result.transpose(0, 2, 1, 3)
+
+
+def body(split_maps, tile_start, pattern):
+    if lax.axis_size("ra") == FBN:
+        return kernel_body(split_maps, tile_start, pattern)
+    return plain_body(split_maps, tile_start, pattern)
+
+
 def solution(mesh):
     placed = (P(None, None, "grp", "ra"), P(("grp", "ra"), None), P("grp", "ra"))
     return jax.shard_map(

time: 232 us -> 41.9 us (0.18)
  the two profiles are of different devices: /device:TPU:15 before, /device:TPU:0 now
where the time goes in v2:
time: 41.9 us; the launch traced here: 41.8 us
  Pallas kernels  41.8 us (100%)
    pallas_call x1, Pallas kernels, kernel_body(): pl.pallas_call(functools.partial(power_kernel, n), out_shape=jax.ShapeDty...  38.4 us
    pallas_call x1, Pallas kernels, kernel_body(): pl.pallas_call(finish_kernel, out_shape=jax.ShapeDtypeStruct((n, PAIRS, F...  3.41 us

profile of v2, /device:TPU:0, one launch (start us, length us, event | category | flops | bytes accessed | tf_op | source)
XLA Modules:
  0.0 41.8 jit_solution(4422112888579053206)
XLA Ops:
  0.0 38.4 %shard_map.73.power_in = bf16[16,96,256]{2,1,0:T(8,128)(2,1)} custom-call(s32[1,2]{1,0:T(1,128)} %corner_ref.1, bf16[4,3,512,128]{3,2,1,0:T(8,128)(2,1)} %maps_in.1, f32[2,64,128]{2,1,0:T(8,128)} %constant.8.clone.wy_in, f32[8,256]{1,0:T(8,128)} %constant.9.clone.wx_in, bf16[256,512]{1,0:T(8,128)(2,1)} %constant.10.clone.t1_in, ...), custom_call_target="tpu_custom_call" | custom-call | tf_op jit(solution)/shard_map/pallas_call | solution.py:452
  38.4 3.4 %shard_map.74 = f32[16,6,16,256]{3,2,1,0:T(8,128)} custom-call(s32[16,16]{1,0:T(8,128)} %pattern_in.1, bf16[16,96,256]{2,1,0:T(8,128)(2,1)} %shard_map.73.power_in), custom_call_target="tpu_custom_call" | custom-call | tf_op jit(solution)/shard_map/pallas_call | solution.py:487
